TPU v7x, 128 devices: a whole 4x4x4 slice. The times are simulated.
128 devices in a mesh: dp: 32 (over y, x, core), tensor: 4 (over z).
Axes of the slice: x: 4, y: 4, z: 4, core: 2. Of those that a mesh axis runs over, the one named last changes fastest.
Arguments:
- tokens: bfloat16 [77824, 768], P(('dp', 'tensor')), may hold values from -6 to 6
- prompt_table: float32 [100, 768], replicated, may hold values from -6 to 6
- lengths: int32 [256], P('dp'), may hold values from 1 to 100, as said below
- table_rows: int32 [256, 100], P('dp'), may hold values from 0 to 99
- ln1_gain: float32 [768], replicated, may hold values from 0.1 to 1.9
- ln1_bias: float32 [768], replicated, may hold values from -3 to 3
- w_qkv: float32 [3, 768, 768], P(None, 'dp', 'tensor'), may hold values from -0.21875 to 0.21875
- qv_bias: float32 [2, 768], P(None, 'tensor'), may hold values from -1.5 to 1.5
- w_out: float32 [768, 768], P('tensor', 'dp'), may hold values from -0.875 to 0.875
- out_bias: float32 [768], replicated, may hold values from -3 to 3
- ln2_gain: float32 [768], replicated, may hold values from 0.1 to 1.9
- ln2_bias: float32 [768], replicated, may hold values from -3 to 3
- w_up: float32 [768, 3072], P('dp', 'tensor'), may hold values from -0.21875 to 0.21875
- up_bias: float32 [3072], P('tensor'), may hold values from -3 to 3
- w_down: float32 [3072, 768], P('tensor', 'dp'), may hold values from -0.109375 to 0.109375
- down_bias: float32 [768], replicated, may hold values from -3 to 3
- cotangent: bfloat16 [77824, 768], P(('dp', 'tensor')), may hold values from -6 to 6
Outputs:
- output: bfloat16 [77824, 768], P(('dp', 'tensor'))
- token_grad: float32 [77824, 768], P(('dp', 'tensor'))
- table_grad: float32 [100, 768], replicated
Inputs may be any that keep to these rules, and one draw needn't show every extreme that they name: `lengths`: each image's prompt length is one of 1, 10, 50 and 100; in every draw some image has 100 and some has 1. `table_rows`: only the first lengths[i] slots of image i are used.
All inputs are finite; a program needn't handle non-finite values.
Results may differ from a plain program's by a relative error of at most 0.012.
The roundings to bfloat16 on the way count: a program that leaves them out, or rounds other values in their place, can miss the bound.
Values may be sent and summed in bfloat16 or wider, within the bound.
A program may use at most 128 MiB of HBM per device.

v0:
```python
import functools

import jax
import jax.numpy as jnp
from jax import lax
from jax.experimental import pallas as pl
from jax.experimental.pallas import tpu as pltpu
from jax.sharding import PartitionSpec as P

D = 768
HD = 64
PATCHES = 197
PROMPTS = 100
SEQ = 304
NZ = 4
HZ = 3
QW = 192
FZ = 768
EPSILON = 1e-06
MASKED = -1e30
F32 = jnp.float32
BF = jnp.bfloat16
NN = (((1,), (0,)), ((), ()))
NT = (((1,), (1,)), ((), ()))
TN = (((0,), (0,)), ((), ()))
MESH = pl.DeviceIdType.MESH
DMA = pltpu.SemaphoreType.DMA
ORDERS = ((0, 1, 2), (1, 2, 0), (2, 0, 1))
NEAR_FIRST = (1, 3, 2)
TAIL = 192


def mm(a, b, dims=NN):
    return lax.dot_general(a, b, dims, preferred_element_type=F32)


def exact(a, b, dims=NN):
    return lax.dot_general(a, b, dims, precision=lax.Precision.HIGHEST, preferred_element_type=F32)


def gelu_pair(u):
    t = 1.0 / (1.0 + (0.3275911 * 0.7071067811865476) * jnp.abs(u))
    e = jnp.exp(-0.5 * (u * u))
    poly = t * (0.254829592 + t * (-0.284496736 + t * (1.421413741 + t * (-1.453152027 + t * 1.061405429))))
    half = 0.5 * poly * e
    cdf = jnp.where(u >= 0, 1.0 - half, half)
    return u * cdf, cdf + u * (0.3989422804014327 * e)


def stats(h):
    c = h - jnp.mean(h, axis=-1, keepdims=True)
    r = lax.rsqrt(jnp.mean(c * c, axis=-1, keepdims=True) + EPSILON)
    return c * r, r


def norm_back(g, n, r, gain):
    e = g * gain
    return r * (e - jnp.mean(e, axis=-1, keepdims=True) - n * jnp.mean(e * n, axis=-1, keepdims=True))


class Net:
    def __init__(self):
        dp = lax.axis_index("dp")
        self.core = lax.rem(dp, 2)
        self.chip = lax.div(dp, 2)
        self.at = (lax.rem(self.chip, 4), lax.div(self.chip, 4), lax.axis_index("tensor"))

    def device(self, at, core):
        return ((at[1] * 4 + at[0]) * 2 + core, at[2])

    def moved(self, axis, step):
        at = list(self.at)
        at[axis] = lax.rem(at[axis] + step, 4)
        return tuple(at)

    def sibling(self):
        return self.device(self.at, 1 - self.core)

    def along(self, axis, step):
        return self.device(self.moved(axis, step), self.core)

    def plane(self, i):
        return (lax.rem(self.chip + i, 16) * 2 + self.core, self.at[2])

    def greet(self):
        sem = pltpu.get_barrier_semaphore()
        peers = [self.sibling()] + [self.plane(i) for i in range(1, 16)] + [self.along(2, d) for d in (1, 2, 3)]
        for peer in peers:
            pl.semaphore_signal(sem, inc=1, device_id=peer, device_id_type=MESH)
        return len(peers)


def remote(src, dst, send, recv, to):
    return pltpu.make_async_remote_copy(src_ref=src, dst_ref=dst, send_sem=send, recv_sem=recv, device_id=to, device_id_type=MESH)


class Part:
    def __init__(self, net, G, where, sems):
        self.net, self.G, self.where, self.sems = net, G, where, sems

    def view(self, p, phase, at, half=None):
        at = list(at)
        for axis in ORDERS[p][:phase]:
            at[axis] = slice(None)
        if half is not None:
            at[ORDERS[p][0]] = pl.ds(2 * half, 2)
        return self.G.at[(*self.where, at[2], at[1], at[0], p)]

    def start(self, phase, send, recv, ds=NEAR_FIRST):
        for d in ds:
            for p in range(3):
                ref = self.view(p, phase, self.net.at)
                remote(ref, ref, self.sems.at[send], self.sems.at[recv], self.net.along(ORDERS[p][phase], d)).start()

    def pass_along(self, send, recv):
        for p in range(3):
            for d in (1, 3):
                axis = ORDERS[p][2]
                ref = self.view(p, 2, self.net.moved(axis, 4 - d), d // 2)
                remote(ref, ref, self.sems.at[send], self.sems.at[recv], self.net.along(axis, d)).start()

    def bulk(self, blocks):
        all_ = slice(None)
        piece = {9: (0, 0, pl.ds(0, 3)), 36: (0, all_, pl.ds(0, 3)), 48: (0,), 96: (pl.ds(0, 2),), 144: (all_, all_, pl.ds(0, 3)), 192: ()}[blocks]
        return self.G.at[(*self.where, *piece)]

    def wait(self, blocks, sem):
        ref = self.bulk(blocks)
        remote(ref, ref, self.sems.at[sem], self.sems.at[sem], self.net.sibling()).wait_recv()

    def wait_sent(self, blocks, sem):
        ref = self.bulk(blocks)
        remote(ref, ref, self.sems.at[sem], self.sems.at[sem], self.net.sibling()).wait_send()

    def slab(self, p, d, send, recv):
        ref = self.view(p, 2, self.net.moved(ORDERS[p][2], 4 - d) if d else self.net.at)
        return remote(ref, ref, self.sems.at[send], self.sems.at[recv], self.net.sibling())

    def whole(self, send, recv):
        ref = self.bulk(192)
        return remote(ref, ref, self.sems.at[send], self.sems.at[recv], self.net.sibling())


def compute(rows, lens_h, tok_h, table_h, trows_h, g1_h, b1_h, ob_h, g2_h, b2_h, db_h, cot_h, qvb_h, upb_h, wq_h, wo_h, wu_h, wd_h,
            out_h, tgrad_h, pgrad_h,
            lens, tok, table, trows, g1_, b1_, ob_, g2_, b2_, db_, cot, qvb, upb, wq, wo, wu, wd,
            inp, fin, qkv, probs, att, mid, sin, hid, dup, dmid, dml, dat, dqkv, out, tgrad,
            GA, GB, GC, stage, other, bias, part, half, slots, zslots, final, pbuf, isem, psem, gsem, tsem, osem):
    images = rows // SEQ
    net = Net()
    t = net.at[2]
    n_peers = net.greet()

    loads = []
    for k, (src, dst) in enumerate(((wq_h, wq), (wo_h, wo), (wu_h, wu), (wd_h, wd), (lens_h, lens), (trows_h, trows), (table_h, table),
                                    (tok_h, tok), (qvb_h, qvb), (upb_h, upb), (g1_h, g1_), (b1_h, b1_), (ob_h, ob_), (g2_h, g2_),
                                    (b2_h, b2_), (db_h, db_), (cot_h, cot))):
        loads.append(pltpu.make_async_copy(src, dst, isem.at[k]))
    for load in loads:
        load.start()
    for load in loads[:4]:
        load.wait()
    stage[0] = jnp.concatenate([wq[0], wq[1], wq[2], wo[...]], axis=1)
    stage[1] = wu[...]
    stage[2] = wd[...]
    for load in loads[4:12]:
        load.wait()

    hots, lives = [], []
    for i in range(images):
        length = lens[t * images + i]
        base = jnp.concatenate([trows[pl.ds(t * images + i, 1), :], jnp.full((1, 384 - PROMPTS), -1, jnp.int32)], axis=1)
        slot = pltpu.roll(base, PATCHES - TAIL, 1)[:, :SEQ - TAIL]
        place = lax.broadcasted_iota(jnp.int32, (1, SEQ - TAIL), 1) + TAIL
        slot = jnp.where((place >= PATCHES) & (place < PATCHES + length), slot, -1)
        hots.append((lax.broadcasted_iota(jnp.int32, (PROMPTS, SEQ - TAIL), 0) == slot).astype(F32))
        place = lax.broadcasted_iota(jnp.int32, (SEQ - TAIL, 1), 0) + TAIL
        lives.append((place >= PATCHES) & (place < PATCHES + length))
    row = lambda ref: ref[...].reshape(1, D)
    for i in range(images):
        lo, hi = pl.ds(i * SEQ, TAIL), pl.ds(i * SEQ + TAIL, SEQ - TAIL)
        inp[lo, :] = tok[lo, :].astype(F32)
        inp[hi, :] = jnp.where(lives[i], exact(hots[i], table[...], TN), tok[hi, :].astype(F32))
        rs = pl.ds(i * SEQ, SEQ)
        fin[rs, :] = (stats(inp[rs, :])[0] * row(g1_) + row(b1_)).astype(BF)
    bias[t] = jnp.concatenate([qvb[0:1, :], jnp.zeros((1, QW), F32), qvb[1:2, :], jnp.zeros((1, 64), F32), upb[...].reshape(1, FZ)], axis=1)

    a = Part(net, GA, (net.core,), gsem)
    b = Part(net, GB, (net.core,), gsem)
    c = Part(net, GC, (slice(None), net.core, slice(None)), gsem)

    def third(j):
        return Part(net, GC, (j, net.core, slice(None)), gsem)

    pl.semaphore_wait(pltpu.get_barrier_semaphore(), n_peers)

    def pre(m):
        return remote(stage.at[m], other.at[m], psem.at[0, m], psem.at[1, m], net.sibling())

    def assemble(m, G, where, first, width):
        cs = pl.ds(pl.multiple_of(first + net.core * width, 128), width)
        mine, theirs = stage[m, :, cs], other[m, :, cs]
        own = net.core == 0
        both = jnp.concatenate([jnp.where(own, mine, theirs), jnp.where(own, theirs, mine)], axis=0).astype(BF)
        x, y, z = net.at
        for p in range(3):
            for w, lo in where:
                hi = lo + G.shape[-1]
                G[(*w, z, y, x, p)] = both[p * 16:(p + 1) * 16, lo:hi]

    def bias_copy(d):
        return remote(bias.at[t], bias.at[t], psem.at[0, 3], psem.at[1, 3], net.along(2, d))

    for m in range(3):
        pre(m).start()
    pre(0).wait_recv()
    assemble(0, GA, [((net.core,), 0)], 0, 256)
    a.start(0, 0, 1)
    assemble(0, GB, [((net.core,), 0)], 512, 128)
    b.start(0, 2, 3)
    for m in (1, 2):
        pre(m).wait_recv()
        assemble(m, GC, [((j, net.core, m - 1), 128 * j) for j in range(3)], 0, 384)
    c.start(0, 4, 5)
    for d in (1, 2, 3):
        bias_copy(d).start()
    a.wait(9, 1)
    a.start(1, 6, 7)
    b.wait(9, 3)
    b.start(1, 8, 9)
    c.wait(9, 5)
    c.start(1, 10, 11)
    a.wait(36, 7)
    for d, r in zip(NEAR_FIRST, (13, 14, 15)):
        a.start(2, 12, r, (d,))
    for p in range(3):
        a.slab(p, 0, 16, 17).start()
    b.wait(36, 9)
    b.start(2, 18, 19)
    c.wait(36, 11)
    for j in range(3):
        third(j).start(2, 22 + 6 * j, 23 + 6 * j, (1, 3))
    for d, r in zip(NEAR_FIRST, (13, 14, 15)):
        a.wait(48, r)
        for p in range(3):
            a.slab(p, d, 16, 17).start()
    a.wait(192, 17)
    remote(bias.at[pl.ds(0, 3)], bias.at[pl.ds(0, 3)], psem.at[0, 3], psem.at[1, 3], net.sibling()).wait()

    def w_a(z):
        return jnp.concatenate([GA[core, z].reshape(D, 256) for core in range(2)], axis=1)

    def w_b(z):
        return jnp.concatenate([GB[core, z].reshape(D, 128) for core in range(2)], axis=1)

    def pair(m, z, j):
        return jnp.concatenate([GC[j, core, m, z].reshape(D, 128) for core in range(2)], axis=1)

    x = fin[...]
    for z in range(NZ):
        qkv[z, :, 0:512] = (mm(x, w_a(z)) + bias[z, :, 0:512]).astype(BF)
    b.wait(144, 19)
    b.whole(20, 21).start()
    b.wait(192, 21)
    last = mm(fin[...], jnp.concatenate([w_b(z)[:, :HD] for z in range(NZ)], axis=1))
    for z in range(NZ):
        qkv[z, :, 512:576] = (last[:, z * 64:(z + 1) * 64] + bias[z, :, 512:576]).astype(BF)

    def attend(z):
        for i in range(images):
            rs = pl.ds(i * SEQ, SEQ)
            blk = qkv[z, rs, :]
            alive = lax.broadcasted_iota(jnp.int32, (SEQ - TAIL, 1), 0) + TAIL < PATCHES + lens[t * images + i]
            outs = []
            for h in range(HZ):
                q = (blk[:, h * HD:(h + 1) * HD] * 0.125).astype(BF)
                k = blk[:, QW + h * HD:QW + (h + 1) * HD]
                v = blk[:, 2 * QW + h * HD:2 * QW + (h + 1) * HD]
                s = mm(k, q, NT)
                s = jnp.concatenate([s[:TAIL], jnp.where(alive, s[TAIL:], MASKED)], axis=0)
                e = jnp.exp(s - jnp.max(s, axis=0, keepdims=True))
                p = (e * (1.0 / jnp.sum(e, axis=0, keepdims=True))).astype(BF)
                probs[z, i * HZ + h] = p
                outs.append(mm(p, v, TN).astype(BF))
            att[z, rs, :] = jnp.concatenate(outs, axis=1)

    def onward(j):
        third(j).wait(96, 23 + 6 * j)
        third(j).pass_along(24 + 6 * j, 25 + 6 * j)

    def relay(j):
        third(j).wait(48, 25 + 6 * j)
        third(j).whole(26 + 6 * j, 27 + 6 * j).start()

    onward(0)
    attend(0)
    attend(1)
    onward(1)
    attend(2)
    attend(3)
    onward(2)
    relay(0)

    for load_ in loads[12:]:
        load_.wait()
    wout = jnp.concatenate([w_b(z)[:, HD:] for z in range(NZ)], axis=1)
    for i in range(images):
        rs = pl.ds(i * SEQ, SEQ)
        h = inp[rs, :] + mm(jnp.concatenate([att[z, rs, :] for z in range(NZ)], axis=1), wout, NT) + row(ob_)
        mid[rs, :] = h
        sin[rs, :] = (stats(h)[0] * row(g2_) + row(b2_)).astype(BF)

    relay(1)

    @pl.loop(0, 3)
    def _(j):
        third(j).wait(192, 27 + 6 * j)
        for z in range(NZ):
            ub = jnp.concatenate([bias[z, :, pl.ds(pl.multiple_of(o + j * 128, 128), 128)] for o in (640, 1024)], axis=1)
            u = mm(sin[...], pair(0, z, j)) + ub
            dh = mm(cot[...], pair(1, z, j))
            g, slope = gelu_pair(u)
            here = pl.ds(pl.multiple_of((j * NZ + z) * 256, 256), 256)
            hid[:, here] = g.astype(BF)
            dup[:, here] = (dh * slope).astype(BF)

        @pl.when(j == 0)
        def _():
            relay(2)

    total = None
    for j in range(3):
        w = jnp.concatenate([pair(0, z, j) for z in range(NZ)], axis=1)
        piece = mm(dup[:, j * 1024:(j + 1) * 1024], w, NT)
        total = piece if total is None else total + piece
    dmid[...] = total
    for i in range(images):
        rs = pl.ds(i * SEQ, SEQ)
        n, r = stats(mid[rs, :])
        d = cot[rs, :].astype(F32) + norm_back(dmid[rs, :], n, r, row(g2_))
        dmid[rs, :] = d
        dml[rs, :] = d.astype(BF)
    wout = jnp.concatenate([w_b(z)[:, HD:] for z in range(NZ)], axis=1)
    d = mm(dml[...], wout).astype(BF)
    for z in range(NZ):
        dat[z] = d[:, z * QW:(z + 1) * QW]

    def attend_back(z):
        for i in range(images):
            rs = pl.ds(i * SEQ, SEQ)
            blk = qkv[z, rs, :]
            dab = dat[z, rs, :]
            kt = blk[:, QW:2 * QW].T
            dq, dk, dv = [], [], []
            for h in range(HZ):
                q = blk[:, h * HD:(h + 1) * HD]
                v = blk[:, 2 * QW + h * HD:2 * QW + (h + 1) * HD]
                do = dab[:, h * HD:(h + 1) * HD]
                p = probs[z, i * HZ + h]
                dv.append(mm(p, do).astype(BF))
                pf = p.astype(F32)
                x = mm(v, do, NT) * pf
                ds = (x - pf * jnp.sum(x, axis=0, keepdims=True)).astype(BF)
                dk.append((mm(ds, q) * 0.125).astype(BF))
                dq.append(mm(kt[h * HD:(h + 1) * HD], ds))
            dq = (jnp.concatenate(dq, axis=0).T * 0.125).astype(BF)
            dqkv[z, rs, :] = jnp.concatenate([dq] + dk + dv, axis=1)

    @pl.loop(0, NZ // 2)
    def _(w):
        attend_back(2 * w)
        attend_back(2 * w + 1)

    def d_first(slices):
        w = jnp.concatenate([w for z in range(NZ) for w in (w_a(z), w_b(z)[:, :HD])], axis=1)
        x = jnp.concatenate([jnp.concatenate([dqkv[z, sl, :] for z in range(NZ)], axis=1) for sl in slices], axis=0)
        return mm(x, w, NT)

    tails = [pl.ds(i * SEQ + TAIL, SEQ - TAIL) for i in range(images)]
    n, r = stats(jnp.concatenate([inp[sl, :] for sl in tails], axis=0))
    d = jnp.concatenate([dmid[sl, :] for sl in tails], axis=0) + norm_back(d_first(tails), n, r, row(g1_))
    total = exact(jnp.concatenate(hots, axis=1), d)
    for i, sl in enumerate(tails):
        tgrad[sl, :] = jnp.where(lives[i], 0.0, d[i * (SEQ - TAIL):(i + 1) * (SEQ - TAIL)])
    part[...] = jnp.concatenate([total, jnp.zeros((128 - PROMPTS, D), F32)], axis=0)

    core, chip = net.core, net.chip
    mine = pl.ds(pl.multiple_of(core * 384, 128), 384)
    theirs = pl.ds(pl.multiple_of((1 - core) * 384, 128), 384)
    here = pl.ds(pl.multiple_of(chip * 8, 8), 8)

    def rest(i):
        lo = pl.ds(i * SEQ, TAIL)
        n, r = stats(inp[lo, :])
        tgrad[lo, :] = dmid[lo, :] + norm_back(d_first([lo]), n, r, row(g1_))

    def down():
        @pl.loop(0, images)
        def _(i):
            rs = pl.ds(pl.multiple_of(i * SEQ, 16), SEQ)
            acc = None
            for j in range(3):
                w = jnp.concatenate([pair(1, z, j) for z in range(NZ)], axis=1)
                piece = mm(hid[rs, j * 1024:(j + 1) * 1024], w, NT)
                acc = piece if acc is None else acc + piece
            out[rs, :] = (mid[rs, :] + acc + row(db_)).astype(BF)

    swap = remote(part.at[:, theirs], half, tsem.at[0], tsem.at[1], net.sibling())
    swap.start()
    rest(0)
    swap.wait()
    part[:, mine] = part[:, mine] + half[...]
    for i in range(1, 16):
        dst = lax.rem(chip + i, 16)
        remote(part.at[pl.ds(pl.multiple_of(dst * 8, 8), 8), mine], slots.at[i], tsem.at[2], tsem.at[3], net.plane(i)).start()
    rest(1)
    tout = pltpu.make_async_copy(tgrad, tgrad_h, osem.at[0])
    tout.start()
    down()
    oout = pltpu.make_async_copy(out, out_h, osem.at[1])
    oout.start()
    fifteen = slots.at[pl.ds(1, 15)]
    remote(fifteen, fifteen, tsem.at[2], tsem.at[3], net.sibling()).wait()
    acc = part[here, mine]
    for i in range(1, 16):
        acc = acc + slots[i]
    zslots[t] = acc
    for d in (1, 2, 3):
        remote(zslots.at[t], zslots.at[t], tsem.at[4], tsem.at[5], net.along(2, d)).start()
    three = zslots.at[pl.ds(0, 3)]
    remote(three, three, tsem.at[4], tsem.at[5], net.sibling()).wait()
    final[here, mine] = (zslots[0] + zslots[1]) + (zslots[2] + zslots[3])
    ref = final.at[here, mine]
    for i in range(1, 16):
        remote(ref, ref, tsem.at[6], tsem.at[7], net.plane(i)).start()
    for m in range(3):
        pre(m).wait_send()
    for part_, sems in ((a, (0, 6, 12, 16)), (b, (2, 8, 18, 20))):
        for blocks, sem in zip((9, 36, 144, 192), sems):
            part_.wait_sent(blocks, sem)
    c.wait_sent(9, 4)
    c.wait_sent(36, 10)
    for j in range(3):
        third(j).wait_sent(96, 22 + 6 * j)
        third(j).wait_sent(48, 24 + 6 * j)
        third(j).wait_sent(192, 26 + 6 * j)
    many = final.at[pl.ds(0, 120), mine]
    remote(many, many, tsem.at[6], tsem.at[7], net.sibling()).wait()
    done = remote(final.at[pl.ds(0, 104), mine], final.at[pl.ds(0, 104), mine], tsem.at[8], tsem.at[9], net.sibling())
    done.start()
    done.wait()
    pbuf[...] = final[0:PROMPTS, :]
    pout = pltpu.make_async_copy(pbuf, pgrad_h, osem.at[2])
    pout.start()
    pout.wait()
    tout.wait()
    oout.wait()


def hand_over(pairs, *refs):
    n = len(pairs)
    srcs, dsts, bufs, sem = refs[:n], refs[n:2 * n], refs[2 * n:3 * n], refs[3 * n]
    pieces = []
    for src, dst, buf, rows in zip(srcs, dsts, bufs, pairs):
        for first in range(0, src.shape[0], rows):
            pieces.append((src, dst, buf, pl.ds(first, min(rows, src.shape[0] - first))))
    into = [pltpu.make_async_copy(s.at[r], b.at[r], sem.at[0, k]) for k, (s, d, b, r) in enumerate(pieces)]
    away = [pltpu.make_async_copy(b.at[r], d.at[r], sem.at[1, k]) for k, (s, d, b, r) in enumerate(pieces)]
    for copy in into:
        copy.start()
    for first, second in zip(into, away):
        first.wait()
        second.start()
    for copy in away:
        copy.wait()


def body(tokens, prompt_table, lengths, table_rows, ln1_gain, ln1_bias, w_qkv, qv_bias, w_out, out_bias,
         ln2_gain, ln2_bias, w_up, up_bias, w_down, down_bias, cotangent):
    rows = tokens.shape[0]
    images = rows // SEQ
    any_ = pl.BlockSpec(memory_space=pl.ANY)
    args = (lengths, tokens, prompt_table, table_rows, ln1_gain, ln1_bias, out_bias, ln2_gain, ln2_bias, down_bias, cotangent,
            qv_bias, up_bias, w_qkv, w_out.T, w_up, w_down.T)
    vmem = lambda shape, dtype: pltpu.VMEM(shape, dtype)
    token_out, grad_out, table_out = pl.pallas_call(
        functools.partial(compute, rows),
        out_shape=(jax.ShapeDtypeStruct((rows, D), BF), jax.ShapeDtypeStruct((rows, D), F32), jax.ShapeDtypeStruct((PROMPTS, D), F32)),
        in_specs=[any_] * len(args),
        out_specs=(any_, any_, any_),
        scratch_shapes=[pltpu.SMEM(lengths.shape, lengths.dtype)] + [vmem(v.shape, v.dtype) for v in args[1:]] + [
            vmem((rows, D), F32),
            vmem((rows, D), BF),
            vmem((NZ, rows, 3 * QW), BF),
            vmem((NZ, images * HZ, SEQ, SEQ), BF),
            vmem((NZ, rows, QW), BF),
            vmem((rows, D), F32),
            vmem((rows, D), BF),
            vmem((rows, NZ * FZ), BF),
            vmem((rows, NZ * FZ), BF),
            vmem((rows, D), F32),
            vmem((rows, D), BF),
            vmem((NZ, rows, QW), BF),
            vmem((NZ, rows, 3 * QW), BF),
            vmem((rows, D), BF),
            vmem((rows, D), F32),
            vmem((2, 4, 4, 4, 3, 16, 256), BF),
            vmem((2, 4, 4, 4, 3, 16, 128), BF),
            vmem((3, 2, 2, 4, 4, 4, 3, 16, 128), BF),
            vmem((3, 24, 768), F32),
            vmem((3, 24, 768), F32),
            vmem((NZ, 1, 1408), F32),
            vmem((128, D), F32),
            vmem((128, 384), F32),
            vmem((16, 8, 384), F32),
            vmem((NZ, 8, 384), F32),
            vmem((128, D), F32),
            vmem((PROMPTS, D), F32),
            DMA((len(args),)), DMA((2, 4)), DMA((40,)), DMA((10,)), DMA((3,)),
        ],
        compiler_params=pltpu.CompilerParams(collective_id=1, has_side_effects=True, vmem_limit_bytes=63 * 2**20),
    )(*args)
    outs = (token_out, grad_out, table_out)
    return pl.pallas_call(
        functools.partial(hand_over, (304, 152, PROMPTS)),
        out_shape=tuple(jax.ShapeDtypeStruct(v.shape, v.dtype) for v in outs),
        in_specs=[any_] * 3,
        out_specs=(any_, any_, any_),
        scratch_shapes=[vmem(v.shape, v.dtype) for v in outs] + [DMA((2, 7))],
    )(*outs)


def solution(mesh):
    row = P(("dp", "tensor"), None)
    return jax.shard_map(
        body, mesh=mesh,
        in_specs=(row, P(), P("dp"), P("dp", None), P(), P(), P(None, "dp", "tensor"), P(None, "tensor"), P("tensor", "dp"),
                  P(), P(), P(), P("dp", "tensor"), P("tensor"), P("tensor", "dp"), P(), row),
        out_specs=(row, row, P()), check_vma=False)
```

profile of v0, /device:TPU:1, one launch (start us, length us, event | category | flops | bytes accessed | tf_op | source)
XLA Modules:
  0.0 96.7 jit_solution(6667812666500686680)
XLA Ops:
  0.6 93.1 %shard_map.184 = (bf16[608,768]{1,0:T(8,128)(2,1)}, f32[608,768]{1,0:T(8,128)}, f32[100,768]{1,0:T(8,128)}) custom-call(s32[8]{0:T(128)} %lens_h.1, bf16[608,768]{1,0:T(8,128)(2,1)} %tok_h.1, f32[100,768]{1,0:T(8,128)} %table_h.1, s32[8,100]{1,0:T(8,128)} %trows_h.1, f32[768]{0:T(1024)} %g1_h.1, f32[768]{0:T(1024)} %b1_h.1, f32[768]{0:T(1024)} %ob_h.1, ...), custom_call_target="tpu_custom_call" | custom-call | tf_op jit(solution)/shard_map/pallas_call | solution.py:486
  93.7 2.8 %shard_map.185 = (bf16[608,768]{1,0:T(8,128)(2,1)}, f32[608,768]{1,0:T(8,128)}, f32[100,768]{1,0:T(8,128)}) custom-call(bf16[608,768]{1,0:T(8,128)(2,1)} %get-tuple-element.6.refs_0_, f32[608,768]{1,0:T(8,128)} %get-tuple-element.7.refs_1_, f32[100,768]{1,0:T(8,128)} %get-tuple-element.8.refs_2_), custom_call_target="tpu_custom_call" | custom-call | tf_op jit(solution)/shard_map/pallas_call | solution.py:524
where the time goes:
time: 96.9 us; the launch traced here: 96.7 us
  Pallas kernels  95.9 us (99%)
    pallas_call x1, Pallas kernels, body(): pl.pallas_call(functools.partial(compute, rows), out_shape=(jax.ShapeDtyp...  93.1 us
    pallas_call x1, Pallas kernels, body(): pl.pallas_call(functools.partial(hand_over, (304, 152, PROMPTS)), out_sha...  2.79 us

commit v1 on v0

--- a/solution.py
+++ b/solution.py
@@ -144,7 +144,7 @@
 def compute(rows, lens_h, tok_h, table_h, trows_h, g1_h, b1_h, ob_h, g2_h, b2_h, db_h, cot_h, qvb_h, upb_h, wq_h, wo_h, wu_h, wd_h,
             out_h, tgrad_h, pgrad_h,
             lens, tok, table, trows, g1_, b1_, ob_, g2_, b2_, db_, cot, qvb, upb, wq, wo, wu, wd,
-            inp, fin, qkv, probs, att, mid, sin, hid, dup, dmid, dml, dat, dqkv, out, tgrad,
+            inp, fin, qkv, probs, dscores, att, mid, sin, hid, dup, dmid, dml, dat, dqkv, out, tgrad,
             GA, GB, GC, stage, other, bias, part, half, slots, zslots, final, pbuf, isem, psem, gsem, tsem, osem):
     images = rows // SEQ
     net = Net()
@@ -347,24 +347,39 @@
 
     def attend_back(z):
         for i in range(images):
-            rs = pl.ds(i * SEQ, SEQ)
+            rs, hi = pl.ds(i * SEQ, SEQ), pl.ds(i * SEQ + TAIL, SEQ - TAIL)
             blk = qkv[z, rs, :]
             dab = dat[z, rs, :]
             kt = blk[:, QW:2 * QW].T
             dq, dk, dv = [], [], []
             for h in range(HZ):
-                q = blk[:, h * HD:(h + 1) * HD]
                 v = blk[:, 2 * QW + h * HD:2 * QW + (h + 1) * HD]
                 do = dab[:, h * HD:(h + 1) * HD]
                 p = probs[z, i * HZ + h]
-                dv.append(mm(p, do).astype(BF))
+                dv.append(mm(p[TAIL:], do).astype(BF))
                 pf = p.astype(F32)
                 x = mm(v, do, NT) * pf
                 ds = (x - pf * jnp.sum(x, axis=0, keepdims=True)).astype(BF)
-                dk.append((mm(ds, q) * 0.125).astype(BF))
-                dq.append(mm(kt[h * HD:(h + 1) * HD], ds))
-            dq = (jnp.concatenate(dq, axis=0).T * 0.125).astype(BF)
-            dqkv[z, rs, :] = jnp.concatenate([dq] + dk + dv, axis=1)
+                dscores[z, i * HZ + h] = ds
+                dk.append((mm(ds[TAIL:], blk[:, h * HD:(h + 1) * HD]) * 0.125).astype(BF))
+                dq.append(mm(kt[h * HD:(h + 1) * HD], ds[:, 128:]))
+            dq = (jnp.concatenate(dq, axis=0).T[TAIL - 128:] * 0.125).astype(BF)
+            dqkv[z, hi, :] = jnp.concatenate([dq] + dk + dv, axis=1)
+
+    def attend_back_rest(z):
+        for i in range(images):
+            rs, lo = pl.ds(i * SEQ, SEQ), pl.ds(i * SEQ, TAIL)
+            blk = qkv[z, rs, :]
+            dab = dat[z, rs, :]
+            kt = blk[:, QW:2 * QW].T
+            dq, dk, dv = [], [], []
+            for h in range(HZ):
+                dv.append(mm(probs[z, i * HZ + h, :TAIL, :], dab[:, h * HD:(h + 1) * HD]).astype(BF))
+                ds = dscores[z, i * HZ + h]
+                dk.append((mm(ds[:TAIL], blk[:, h * HD:(h + 1) * HD]) * 0.125).astype(BF))
+                dq.append(mm(kt[h * HD:(h + 1) * HD], ds[:, :256]))
+            dq = (jnp.concatenate(dq, axis=0).T[:TAIL] * 0.125).astype(BF)
+            dqkv[z, lo, :] = jnp.concatenate([dq] + dk + dv, axis=1)
 
     @pl.loop(0, NZ // 2)
     def _(w):
@@ -407,18 +422,17 @@
 
     swap = remote(part.at[:, theirs], half, tsem.at[0], tsem.at[1], net.sibling())
     swap.start()
-    rest(0)
     swap.wait()
     part[:, mine] = part[:, mine] + half[...]
     for i in range(1, 16):
         dst = lax.rem(chip + i, 16)
         remote(part.at[pl.ds(pl.multiple_of(dst * 8, 8), 8), mine], slots.at[i], tsem.at[2], tsem.at[3], net.plane(i)).start()
-    rest(1)
-    tout = pltpu.make_async_copy(tgrad, tgrad_h, osem.at[0])
-    tout.start()
-    down()
-    oout = pltpu.make_async_copy(out, out_h, osem.at[1])
-    oout.start()
+
+    @pl.loop(0, NZ // 2)
+    def _(w):
+        attend_back_rest(2 * w)
+        attend_back_rest(2 * w + 1)
+
     fifteen = slots.at[pl.ds(1, 15)]
     remote(fifteen, fifteen, tsem.at[2], tsem.at[3], net.sibling()).wait()
     acc = part[here, mine]
@@ -427,12 +441,19 @@
     zslots[t] = acc
     for d in (1, 2, 3):
         remote(zslots.at[t], zslots.at[t], tsem.at[4], tsem.at[5], net.along(2, d)).start()
+    rest(0)
+    rest(1)
+    tout = pltpu.make_async_copy(tgrad, tgrad_h, osem.at[0])
+    tout.start()
     three = zslots.at[pl.ds(0, 3)]
     remote(three, three, tsem.at[4], tsem.at[5], net.sibling()).wait()
     final[here, mine] = (zslots[0] + zslots[1]) + (zslots[2] + zslots[3])
     ref = final.at[here, mine]
     for i in range(1, 16):
         remote(ref, ref, tsem.at[6], tsem.at[7], net.plane(i)).start()
+    down()
+    oout = pltpu.make_async_copy(out, out_h, osem.at[1])
+    oout.start()
     for m in range(3):
         pre(m).wait_send()
     for part_, sems in ((a, (0, 6, 12, 16)), (b, (2, 8, 18, 20))):
@@ -492,6 +513,7 @@
             vmem((rows, D), F32),
             vmem((rows, D), BF),
             vmem((NZ, rows, 3 * QW), BF),
+            vmem((NZ, images * HZ, SEQ, SEQ), BF),
             vmem((NZ, images * HZ, SEQ, SEQ), BF),
             vmem((NZ, rows, QW), BF),
             vmem((rows, D), F32),

time: 96.9 us -> 95.1 us (0.981)
  Pallas kernels: 95.9 us -> 94.1 us
    pallas_call x1, Pallas kernels: 93.1 us -> 91.3 us  [body(): pl.pallas_call(functools.partial(compute, rows), out_shape=(jax.ShapeDtyp...]
where the time goes in v1:
time: 95.1 us; the launch traced here: 94.9 us
  Pallas kernels  94.1 us (99%)
    pallas_call x1, Pallas kernels, body(): pl.pallas_call(functools.partial(compute, rows), out_shape=(jax.ShapeDtyp...  91.3 us
    pallas_call x1, Pallas kernels, body(): pl.pallas_call(functools.partial(hand_over, (304, 152, PROMPTS)), out_sha...  2.79 us

profile of v1, /device:TPU:1, one launch (start us, length us, event | category | flops | bytes accessed | tf_op | source)
XLA Modules:
  0.0 94.9 jit_solution(4445977413838137570)
XLA Ops:
  0.6 91.3 %shard_map.184 = (bf16[608,768]{1,0:T(8,128)(2,1)}, f32[608,768]{1,0:T(8,128)}, f32[100,768]{1,0:T(8,128)}) custom-call(s32[8]{0:T(128)} %lens_h.1, bf16[608,768]{1,0:T(8,128)(2,1)} %tok_h.1, f32[100,768]{1,0:T(8,128)} %table_h.1, s32[8,100]{1,0:T(8,128)} %trows_h.1, f32[768]{0:T(1024)} %g1_h.1, f32[768]{0:T(1024)} %b1_h.1, f32[768]{0:T(1024)} %ob_h.1, ...), custom_call_target="tpu_custom_call" | custom-call | tf_op jit(solution)/shard_map/pallas_call | solution.py:507
  92.0 2.8 %shard_map.185 = (bf16[608,768]{1,0:T(8,128)(2,1)}, f32[608,768]{1,0:T(8,128)}, f32[100,768]{1,0:T(8,128)}) custom-call(bf16[608,768]{1,0:T(8,128)(2,1)} %get-tuple-element.6.refs_0_, f32[608,768]{1,0:T(8,128)} %get-tuple-element.7.refs_1_, f32[100,768]{1,0:T(8,128)} %get-tuple-element.8.refs_2_), custom_call_target="tpu_custom_call" | custom-call | tf_op jit(solution)/shard_map/pallas_call | solution.py:546

commit v2 on v1

--- a/solution.py
+++ b/solution.py
@@ -27,6 +27,8 @@
 DMA = pltpu.SemaphoreType.DMA
 ORDERS = ((0, 1, 2), (1, 2, 0), (2, 0, 1))
 NEAR_FIRST = (1, 3, 2)
+FAR_FIRST = (2, 1, 3)
+PLANE = (10, 6, 9, 11, 14, 2, 8, 5, 7, 13, 15, 1, 3, 4, 12)
 TAIL = 192
 
 
@@ -84,7 +86,7 @@
 
     def greet(self):
         sem = pltpu.get_barrier_semaphore()
-        peers = [self.sibling()] + [self.plane(i) for i in range(1, 16)] + [self.along(2, d) for d in (1, 2, 3)]
+        peers = [self.plane(i) for i in PLANE] + [self.along(2, d) for d in FAR_FIRST] + [self.sibling()]
         for peer in peers:
             pl.semaphore_signal(sem, inc=1, device_id=peer, device_id_type=MESH)
         return len(peers)
@@ -215,21 +217,21 @@
         pre(m).start()
     pre(0).wait_recv()
     assemble(0, GA, [((net.core,), 0)], 0, 256)
-    a.start(0, 0, 1)
+    a.start(0, 0, 1, FAR_FIRST)
     assemble(0, GB, [((net.core,), 0)], 512, 128)
-    b.start(0, 2, 3)
+    b.start(0, 2, 3, FAR_FIRST)
     for m in (1, 2):
         pre(m).wait_recv()
         assemble(m, GC, [((j, net.core, m - 1), 128 * j) for j in range(3)], 0, 384)
-    c.start(0, 4, 5)
+    c.start(0, 4, 5, FAR_FIRST)
     for d in (1, 2, 3):
         bias_copy(d).start()
     a.wait(9, 1)
-    a.start(1, 6, 7)
+    a.start(1, 6, 7, FAR_FIRST)
     b.wait(9, 3)
-    b.start(1, 8, 9)
+    b.start(1, 8, 9, FAR_FIRST)
     c.wait(9, 5)
-    c.start(1, 10, 11)
+    c.start(1, 10, 11, FAR_FIRST)
     a.wait(36, 7)
     for d, r in zip(NEAR_FIRST, (13, 14, 15)):
         a.start(2, 12, r, (d,))
@@ -424,7 +426,7 @@
     swap.start()
     swap.wait()
     part[:, mine] = part[:, mine] + half[...]
-    for i in range(1, 16):
+    for i in PLANE:
         dst = lax.rem(chip + i, 16)
         remote(part.at[pl.ds(pl.multiple_of(dst * 8, 8), 8), mine], slots.at[i], tsem.at[2], tsem.at[3], net.plane(i)).start()
 
@@ -439,7 +441,7 @@
     for i in range(1, 16):
         acc = acc + slots[i]
     zslots[t] = acc
-    for d in (1, 2, 3):
+    for d in FAR_FIRST:
         remote(zslots.at[t], zslots.at[t], tsem.at[4], tsem.at[5], net.along(2, d)).start()
     rest(0)
     rest(1)
@@ -449,7 +451,7 @@
     remote(three, three, tsem.at[4], tsem.at[5], net.sibling()).wait()
     final[here, mine] = (zslots[0] + zslots[1]) + (zslots[2] + zslots[3])
     ref = final.at[here, mine]
-    for i in range(1, 16):
+    for i in PLANE:
         remote(ref, ref, tsem.at[6], tsem.at[7], net.plane(i)).start()
     down()
     oout = pltpu.make_async_copy(out, out_h, osem.at[1])
@@ -544,11 +546,11 @@
     )(*args)
     outs = (token_out, grad_out, table_out)
     return pl.pallas_call(
-        functools.partial(hand_over, (304, 152, PROMPTS)),
+        functools.partial(hand_over, (160, 160, PROMPTS)),
         out_shape=tuple(jax.ShapeDtypeStruct(v.shape, v.dtype) for v in outs),
         in_specs=[any_] * 3,
         out_specs=(any_, any_, any_),
-        scratch_shapes=[vmem(v.shape, v.dtype) for v in outs] + [DMA((2, 7))],
+        scratch_shapes=[vmem(v.shape, v.dtype) for v in outs] + [DMA((2, 9))],
     )(*outs)
 
 

time: 95.1 us -> 95 us (level)
  no operation moved by 1% of the time
where the time goes in v2:
time: 95 us; the launch traced here: 94.9 us
  Pallas kernels  94 us (99%)
    pallas_call x1, Pallas kernels, body(): pl.pallas_call(functools.partial(compute, rows), out_shape=(jax.ShapeDtyp...  90.9 us
    pallas_call x1, Pallas kernels, body(): pl.pallas_call(functools.partial(hand_over, (160, 160, PROMPTS)), out_sha...  3.12 us

profile of v2, /device:TPU:1, one launch (start us, length us, event | category | flops | bytes accessed | tf_op | source)
XLA Modules:
  0.0 94.9 jit_solution(17892645448842317877)
XLA Ops:
  0.6 90.9 %shard_map.184 = (bf16[608,768]{1,0:T(8,128)(2,1)}, f32[608,768]{1,0:T(8,128)}, f32[100,768]{1,0:T(8,128)}) custom-call(s32[8]{0:T(128)} %lens_h.1, bf16[608,768]{1,0:T(8,128)(2,1)} %tok_h.1, f32[100,768]{1,0:T(8,128)} %table_h.1, s32[8,100]{1,0:T(8,128)} %trows_h.1, f32[768]{0:T(1024)} %g1_h.1, f32[768]{0:T(1024)} %b1_h.1, f32[768]{0:T(1024)} %ob_h.1, ...), custom_call_target="tpu_custom_call" | custom-call | tf_op jit(solution)/shard_map/pallas_call | solution.py:509
  91.6 3.1 %shard_map.185 = (bf16[608,768]{1,0:T(8,128)(2,1)}, f32[608,768]{1,0:T(8,128)}, f32[100,768]{1,0:T(8,128)}) custom-call(bf16[608,768]{1,0:T(8,128)(2,1)} %get-tuple-element.6.refs_0_, f32[608,768]{1,0:T(8,128)} %get-tuple-element.7.refs_1_, f32[100,768]{1,0:T(8,128)} %get-tuple-element.8.refs_2_), custom_call_target="tpu_custom_call" | custom-call | tf_op jit(solution)/shard_map/pallas_call | solution.py:548
